TPU v7x, 256 devices: a whole 4x4x8 slice. The times are simulated.
256 devices in a mesh: lon: 64 (over x_hi, y, z), dp: 4 (over x_lo, core).
Axes of the slice: x: 4 (x_hi: 2, x_lo: 2; x = x_hi * 2 + x_lo), y: 4, z: 8, core: 2. Of those that a mesh axis runs over, the one named last changes fastest.
Arguments:
- fields: bfloat16 [4, 77, 512, 128], P('dp', None, 'lon'), may hold values from -6 to 6
- targets: bfloat16 [4, 77, 512, 128], P('dp', None, 'lon'), as said below
- land_sea: int32 [512, 128], P('lon'), may hold values 0 or 1
- clip_level: int32 [77], replicated, may hold values from 2 to 63
- stem_weight: bfloat16 [200, 77], P('dp'), may hold values from -0.625 to 0.625
- dw_kernel: bfloat16 [200, 49], P('dp'), may hold values from -0.875 to 0.875
- up_weight: bfloat16 [200, 800], P('dp'), may hold values from -0.4375 to 0.4375
- down_weight: bfloat16 [800, 200], P('dp'), may hold values from -0.21875 to 0.21875
- head_weight: bfloat16 [200, 77], P('dp'), may hold values from -0.4375 to 0.4375
Outputs:
- stem_weight_gradient: float32 [200, 77], P('dp')
- grad_kernel: float32 [200, 49], P('dp')
- grad_up: float32 [200, 800], P('dp')
- grad_down: float32 [800, 200], P('dp')
- grad_head: float32 [200, 77], P('dp')
- loss: float32 [], replicated
- field_sensitivity: float32 [4, 77, 512, 128], P('dp', None, 'lon')
Inputs may be any that keep to these rules, and one draw needn't show every extreme that they name: targets are real-valued ocean fields between -8 and 8.
All inputs are finite; a program needn't handle non-finite values. No bound on the sum of `land_sea` on one device may be relied on, other than what follows from the above.
Results may differ from a plain program's by a relative error of at most 0.011.
Values may be sent and summed in bfloat16 or wider, within the bound.
A program may use at most 64 MiB of HBM per device.

v0:
```python
import jax
import jax.numpy as jnp
from jax import lax
from jax.sharding import PartitionSpec as P

KERNEL_SIDE = 7
KERNEL_SPACING = 2
HALO = 6


gelu_scale = 0.7978845608


def padded_2(cells, sides, width):
    for axis, dim in sides:
        count = lax.axis_size(axis)
        head = lax.slice_in_dim(cells, 0, width, axis=dim)
        tail = lax.slice_in_dim(cells, cells.shape[dim] - width, cells.shape[dim], axis=dim)
        cells = jnp.concatenate(
            [
                lax.ppermute(tail, axis, [(i, (i + 1) % count) for i in range(count)]),
                cells,
                lax.ppermute(head, axis, [((i + 1) % count, i) for i in range(count)]),
            ],
            axis=dim,
        )
    return cells


def gelu_pair(values):
    inner = gelu_scale * (values + 0.044715 * values**3)
    tanh_val = jnp.tanh(inner)
    act = 0.5 * values * (1.0 + tanh_val)
    slope = 0.5 * (1.0 + tanh_val) + 0.5 * values * (1.0 - tanh_val**2) * gelu_scale * (
        1.0 + 3.0 * 0.044715 * values**2
    )
    return (act, slope)


def tap_list():
    return [
        (
            (first_operand - KERNEL_SIDE // 2) * KERNEL_SPACING,
            (second_operand - KERNEL_SIDE // 2) * KERNEL_SPACING,
        )
        for first_operand in range(KERNEL_SIDE)
        for second_operand in range(KERNEL_SIDE)
    ]


def shards(
    fields,
    targets,
    land_sea,
    clip_level,
    stem_weight,
    dw_kernel,
    up_weight,
    down_weight,
    head_weight,
):
    stem_full, kernel_full, up_full, head_full, down_full = (
        lax.all_gather(stem_weight, "dp", axis=0, tiled=True),
        lax.all_gather(dw_kernel, "dp", axis=0, tiled=True),
        lax.all_gather(up_weight, "dp", axis=0, tiled=True),
        lax.all_gather(head_weight, "dp", axis=0, tiled=True),
        lax.all_gather(down_weight, "dp", axis=0, tiled=True),
    )
    columns = fields.shape[2]
    lat_rows = fields.shape[3]
    f32 = jnp.float32
    kern32 = kernel_full.astype(f32)

    def kernel_window(source, lon_start, lat_start, width):
        return source[:, :, lon_start : lon_start + width, lat_start : lat_start + lat_rows]

    stem_out = jnp.einsum("cv,svla->scla", stem_full, fields, preferred_element_type=f32).astype(
        jnp.bfloat16
    )
    padded = padded_2(stem_out, (("lon", 2),), HALO)
    padded = jnp.pad(padded, ((0, 0), (0, 0), (0, 0), (HALO, HALO)))
    mixed = jnp.zeros(stem_out.shape, f32)
    for index, (lon_off, lat_off) in enumerate(tap_list()):
        mixed = mixed + kern32[None, :, index, None, None] * kernel_window(
            padded, HALO + lon_off, HALO + lat_off, columns
        ).astype(f32)
    centred = mixed - jnp.mean(mixed, axis=1, keepdims=True)
    rstd = lax.rsqrt(jnp.mean(centred * centred, axis=1, keepdims=True) + 1e-06)
    normed = centred * rstd
    normed_half = normed.astype(jnp.bfloat16)
    hidden_pre = jnp.einsum("cf,scla->sfla", up_full, normed_half, preferred_element_type=f32)
    act, slope = gelu_pair(hidden_pre)
    act_half = act.astype(jnp.bfloat16)
    branch = jnp.einsum("fc,sfla->scla", down_full, act_half, preferred_element_type=f32)
    block_out = (stem_out.astype(f32) + branch).astype(jnp.bfloat16)
    predicted = jnp.einsum("cv,scla->svla", head_full, block_out, preferred_element_type=f32)
    ocean = land_sea.astype(f32)
    misfit = (predicted - targets.astype(f32)) * ocean[None, None]
    squares = jnp.sum(misfit * misfit, axis=(0, 2, 3))
    ocean_local = fields.shape[0] * jnp.sum(ocean)
    squares, ocean_count = lax.psum((squares, ocean_local), ("lon", "dp"))
    threshold = clip_level.astype(f32) / 16.0
    mean_error = squares / ocean_count
    loss = jnp.sum(threshold * jnp.log(1.0 + mean_error / threshold))
    factor = 2.0 / (ocean_count * (1.0 + mean_error / threshold))
    pred_grad = (misfit * factor[None, :, None, None]).astype(jnp.bfloat16)
    g_head = jnp.einsum("scla,svla->cv", block_out, pred_grad, preferred_element_type=f32)
    block_grad = jnp.einsum("cv,svla->scla", head_full, pred_grad, preferred_element_type=f32)
    block_half = block_grad.astype(jnp.bfloat16)
    g_down = jnp.einsum("sfla,scla->fc", act_half, block_half, preferred_element_type=f32)
    hidden_gradient = jnp.einsum("fc,scla->sfla", down_full, block_half, preferred_element_type=f32)
    pre_half = (hidden_gradient * slope).astype(jnp.bfloat16)
    g_up = jnp.einsum("scla,sfla->cf", normed_half, pre_half, preferred_element_type=f32)
    normed_grad = jnp.einsum("cf,sfla->scla", up_full, pre_half, preferred_element_type=f32)
    mixed_half = (
        rstd
        * (
            normed_grad
            - jnp.mean(normed_grad, axis=1, keepdims=True)
            - normed * jnp.mean(normed_grad * normed, axis=1, keepdims=True)
        )
    ).astype(jnp.bfloat16)
    mixed_wide = mixed_half.astype(f32)
    kern_terms = []
    for index, (lon_off, lat_off) in enumerate(tap_list()):
        kern_terms.append(
            jnp.sum(
                mixed_wide
                * kernel_window(padded, HALO + lon_off, HALO + lat_off, columns).astype(f32),
                axis=(0, 2, 3),
            )
        )
    g_kern = jnp.stack(kern_terms, axis=1)
    back_pad = padded_2(mixed_half, (("lon", 2),), HALO)
    back_pad = jnp.pad(back_pad, ((0, 0), (0, 0), (0, 0), (HALO, HALO)))
    back = jnp.zeros(block_grad.shape, f32)
    for index, (lon_off, lat_off) in enumerate(tap_list()):
        back = back + kern32[None, :, index, None, None] * kernel_window(
            back_pad, HALO - lon_off, HALO - lat_off, columns
        ).astype(f32)
    stem_half = (block_grad + back).astype(jnp.bfloat16)
    g_stem = jnp.einsum("scla,svla->cv", stem_half, fields, preferred_element_type=f32)
    field_sensitivity = (
        jnp.einsum("cv,scla->svla", stem_full, stem_half, preferred_element_type=f32) * ocean_count
    )
    local_gradients = (g_stem, g_kern, g_up, g_down, g_head)
    summed = lax.psum(
        (
            local_gradients[0],
            local_gradients[1],
            local_gradients[2],
            local_gradients[3],
            local_gradients[4],
        ),
        "lon",
    )
    shares = (
        lax.psum_scatter(summed[0], "dp", scatter_dimension=0, tiled=True),
        lax.psum_scatter(summed[1], "dp", scatter_dimension=0, tiled=True),
        lax.psum_scatter(summed[2], "dp", scatter_dimension=0, tiled=True),
        lax.psum_scatter(summed[3], "dp", scatter_dimension=0, tiled=True),
        lax.psum_scatter(summed[4], "dp", scatter_dimension=0, tiled=True),
    )
    return (shares[0], shares[1], shares[2], shares[3], shares[4], loss, field_sensitivity)


def solution(mesh):
    placed = (
        P("dp", None, "lon", None),
        P("dp", None, "lon", None),
        P("lon", None),
        P(),
        P("dp", None),
        P("dp", None),
        P("dp", None),
        P("dp", None),
        P("dp", None),
    )
    return jax.shard_map(
        shards,
        mesh=mesh,
        in_specs=placed,
        out_specs=(
            P("dp", None),
            P("dp", None),
            P("dp", None),
            P("dp", None),
            P("dp", None),
            P(),
            P("dp", None, "lon", None),
        ),
        check_vma=False,
    )
```

profile of v0, /device:TPU:6, one launch (start us, length us, event | category | flops | bytes accessed | tf_op | source)
XLA Modules:
  0.0 962.1 jit_solution(15585865789968552278)
XLA Ops:
  7.2 5.5 all-gather
  12.7 1.2 fusion.43
  14.8 1.9 collective-permute-start
  16.7 7.2 collective-permute-start.1
  24.0 5.4 all-gather.1
  29.4 1.3 fusion.217
  30.8 1.8 fusion.216
  33.7 5.4 all-gather.3
  39.1 6.8 all-gather.2
  61.6 1.6 copy.86
  63.2 1.5 copy.85
  64.7 1.5 copy.84
  66.2 1.6 copy.83
  67.8 1.6 copy.82
  69.3 1.6 copy.81
  70.9 1.5 copy.80
  72.4 1.6 copy.79
  74.0 1.6 copy.78
  75.5 1.5 copy.77
  77.1 1.5 copy.76
  78.6 1.5 copy.75
  80.1 1.5 copy.74
  81.7 1.6 copy.73
  83.3 1.5 copy.72
  99.6 6.7 all_gather.18
  107.8 8.7 fusion.211
  117.3 1.4 fusion.40
  119.7 75.7 %all-reduce.9 = (f32[77]{0:T(128)S(1)}, f32[]{:T(128)}) all-reduce(f32[77]{0:T(128)S(1)} %get-tuple-element.155, f32[]{:T(128)} %convert_reduce_fusion), channel_id=1, replica_groups=mesh['lon'=64,'dp'=4] {'lon','dp'}, use_global_device_ids=true, to_apply=%region_5.6 | all-reduce | flops 78 | bytes 624 | tf_op jit(solution)/shard_map/psum | solution.py:101
  197.2 2.0 convolution_bitcast_fusion.2
  200.4 4.1 fusion.28
  204.5 4.4 fusion.12
  210.0 4.1 fusion.167
  214.2 1.6 fusion.166
  215.8 4.1 fusion.168
  220.9 4.5 collective-permute-start.3
  225.3 3.2 fusion.165
  228.5 9.2 stack.199
  237.7 1.6 fusion.31
  241.2 9.4 add_convert_fusion
  250.9 14.4 %fusion.209 = (f32[64,77]{1,0:T(8,128)S(1)}, f32[64,77]{1,0:T(8,128)S(1)}, f32[64,800]{1,0:T(8,128)S(1)}) fusion(f32[200,77]{1,0:T(8,128)S(1)} %convolution_bitcast_fusion.3, f32[200,77]{1,0:T(8,128)S(1)} %copy-done.13, f32[200,800]{1,0:T(8,128)S(1)} %copy-done.8), kind=kCustom, calls=%all-reduce-scatter.3 | all-reduce-scatter fusion | flops 244225 | bytes 1008448
  265.3 1.9 collective-permute-start.5
  267.2 12.4 %all-reduce.3 = f32[200,49]{0,1:T(8,128)S(1)} all-reduce(f32[200,49]{0,1:T(8,128)S(1)} %copy-done.17), channel_id=3, replica_groups=mesh['lon'=64,'dp'=4] {'dp'}, use_global_device_ids=true, to_apply=%region_60.61.clone | all-reduce | flops 9800 | bytes 78400
  279.7 1.9 collective-permute-start.6
  281.6 1.9 collective-permute-start.4
  287.0 359.0 %all-reduce.10 = (f32[50,77]{1,0:T(8,128)}, f32[50,49]{0,1:T(8,128)S(1)}, f32[50,77]{1,0:T(8,128)}) all-reduce(f32[50,77]{1,0:T(8,128)S(1)} %constant_dynamic-slice_fusion.2, f32[50,49]{0,1:T(8,128)S(1)} %constant_dynamic-slice_fusion.3, f32[50,77]{1,0:T(8,128)S(1)} %constant_dynamic-slice_fusion), channel_id=1, replica_groups=mesh['lon'=64,'dp'=4] {'lon'}, use_global_device_ids=true, to_apply=%region_8.9 | all-reduce | flops 10150 | bytes 81200 | tf_op jit(solution)/shard_map/psum | solution.py:147
  646.8 305.2 %all-reduce.15.cloned.1.call-done = (f32[50,800]{1,0:T(8,128)}, f32[200,200]{1,0:T(8,128)}) async-done(((f32[50,800]{1,0:T(8,128)}, f32[200,200]{1,0:T(8,128)}), (f32[50,800]{1,0:T(8,128)}, f32[200,200]{1,0:T(8,128)})) %all-reduce.15.cloned.1.call-update) | async-done | bytes 320016 | tf_op jit(solution)/shard_map/psum | solution.py:147
  952.0 1.6 copy.116
  953.6 1.6 copy.117
  (209 shorter events, 44.9 us)
Async XLA Ops:
  7.2 277.4 %reduce-scatter.9.cloned.1.call-start = ((), (), s32[]{:S(2)}) async-start(), calls=%async_computation.1 | async-start | bytes 1024000 | tf_op jit(solution)/shard_map/reduce_scatter | solution.py:161
  13.9 103.4 %copy-start = (bf16[1,200,8,128]{3,1,2,0:T(8,128)(2,1)}, bf16[1,200,8,128]{3,1,2,0:T(8,128)(2,1)S(1)}, u32[]{:S(2)}) copy-start(bf16[1,200,8,128]{3,1,2,0:T(8,128)(2,1)S(1)} %fusion.43) | copy-start | bytes 1228804
  14.8 91.5 %collective-permute-start = (bf16[1,200,6,128]{3,1,2,0:T(8,128)(2,1)}, bf16[1,200,6,128]{3,1,2,0:T(8,128)(2,1)S(1)}, u32[]{:S(2)}, u32[]{:S(2)}) collective-permute-start(bf16[1,200,6,128]{3,1,2,0:T(8,128)(2,1)} %get-tuple-element.102), channel_id=1, source_target_pairs={{0,4},{4,8},{8,12},{12,16},{16,20},{20,24},{24,28},{28,32},{32,36}... | collective-permute-start | bytes 921608 | tf_op jit(solution)/shard_map/ppermute | solution.py:21
  16.7 89.6 %collective-permute-start.1 = (bf16[1,200,6,128]{3,1,2,0:T(8,128)(2,1)}, bf16[1,200,6,128]{3,1,2,0:T(8,128)(2,1)S(1)}, u32[]{:S(2)}, u32[]{:S(2)}) collective-permute-start(bf16[1,200,6,128]{3,1,2,0:T(8,128)(2,1)} %get-tuple-element.103), channel_id=1, source_target_pairs={{4,0},{8,4},{12,8},{16,12},{20,16},{24,20},{28,24},{32,28},{36,32}... | collective-permute-start | bytes 921608 | tf_op jit(solution)/shard_map/ppermute | solution.py:23
  33.7 51.1 %copy-start.16 = (f32[200,1]{1,0:T(8,128)S(1)}, f32[200,1]{1,0:T(8,128)}, u32[]{:S(2)}) copy-start(f32[200,1]{1,0:T(8,128)} %get-tuple-element.104) | copy-start | bytes 2404
  39.1 58.0 %copy-start.61 = (u32[256]{0:T(256)S(1)}, u32[256]{0:T(256)}, u32[]{:S(2)}) copy-start(u32[256]{0:T(256)} %constant.42) | copy-start | bytes 3076
  46.9 52.8 %copy-start.19 = (bf16[200,200]{1,0:T(8,128)(2,1)S(1)}, bf16[200,200]{1,0:T(8,128)(2,1)}, u32[]{:S(2)}) copy-start(bf16[200,200]{1,0:T(8,128)(2,1)} %param.16) | copy-start | bytes 240004
  50.8 56.6 %copy-start.22 = (f32[200,1]{0,1:T(1,128)}, f32[200,1]{0,1:T(1,128)S(1)}, u32[]{:S(2)}) copy-start(f32[200,1]{0,1:T(1,128)S(1)} %copy.69) | copy-start | bytes 2404
  51.8 55.6 %copy-start.23 = (f32[200,1]{0,1:T(1,128)}, f32[200,1]{0,1:T(1,128)S(1)}, u32[]{:S(2)}) copy-start(f32[200,1]{0,1:T(1,128)S(1)} %copy.68) | copy-start | bytes 2404
  52.8 54.7 %copy-start.24 = (f32[200,1]{0,1:T(1,128)}, f32[200,1]{0,1:T(1,128)S(1)}, u32[]{:S(2)}) copy-start(f32[200,1]{0,1:T(1,128)S(1)} %copy.67) | copy-start | bytes 2404
  53.7 53.7 %copy-start.25 = (f32[200,1]{0,1:T(1,128)}, f32[200,1]{0,1:T(1,128)S(1)}, u32[]{:S(2)}) copy-start(f32[200,1]{0,1:T(1,128)S(1)} %copy.66) | copy-start | bytes 2404
  54.7 52.7 %copy-start.26 = (f32[200,1]{0,1:T(1,128)}, f32[200,1]{0,1:T(1,128)S(1)}, u32[]{:S(2)}) copy-start(f32[200,1]{0,1:T(1,128)S(1)} %copy.65) | copy-start | bytes 2404
  55.7 51.7 %copy-start.27 = (f32[200,1]{0,1:T(1,128)}, f32[200,1]{0,1:T(1,128)S(1)}, u32[]{:S(2)}) copy-start(f32[200,1]{0,1:T(1,128)S(1)} %copy.64) | copy-start | bytes 2404
  56.7 50.8 %copy-start.28 = (f32[200,1]{0,1:T(1,128)}, f32[200,1]{0,1:T(1,128)S(1)}, u32[]{:S(2)}) copy-start(f32[200,1]{0,1:T(1,128)S(1)} %copy.63) | copy-start | bytes 2404
  57.7 49.8 %copy-start.29 = (f32[200,1]{0,1:T(1,128)}, f32[200,1]{0,1:T(1,128)S(1)}, u32[]{:S(2)}) copy-start(f32[200,1]{0,1:T(1,128)S(1)} %copy.108) | copy-start | bytes 2404
  58.7 48.8 %copy-start.30 = (f32[200,1]{0,1:T(1,128)}, f32[200,1]{0,1:T(1,128)S(1)}, u32[]{:S(2)}) copy-start(f32[200,1]{0,1:T(1,128)S(1)} %copy.61) | copy-start | bytes 2404
  59.6 47.8 %copy-start.31 = (f32[200,1]{0,1:T(1,128)}, f32[200,1]{0,1:T(1,128)S(1)}, u32[]{:S(2)}) copy-start(f32[200,1]{0,1:T(1,128)S(1)} %copy.89) | copy-start | bytes 2404
  60.6 46.9 %copy-start.32 = (f32[200,1]{0,1:T(1,128)}, f32[200,1]{0,1:T(1,128)S(1)}, u32[]{:S(2)}) copy-start(f32[200,1]{0,1:T(1,128)S(1)} %copy.88) | copy-start | bytes 2404
  61.6 45.9 %copy-start.33 = (f32[200,1]{0,1:T(1,128)}, f32[200,1]{0,1:T(1,128)S(1)}, u32[]{:S(2)}) copy-start(f32[200,1]{0,1:T(1,128)S(1)} %copy.87) | copy-start | bytes 2404
  96.9 10.7 %copy-start.37 = (f32[200,1]{0,1:T(1,128)S(1)}, f32[200,1]{0,1:T(1,128)}, u32[]{:S(2)}) copy-start(f32[200,1]{0,1:T(1,128)} %copy.76) | copy-start | bytes 2404
  96.9 10.7 %copy-start.38 = (f32[200,1]{0,1:T(1,128)S(1)}, f32[200,1]{0,1:T(1,128)}, u32[]{:S(2)}) copy-start(f32[200,1]{0,1:T(1,128)} %copy.75) | copy-start | bytes 2404
  96.9 10.7 %copy-start.39 = (f32[200,1]{0,1:T(1,128)S(1)}, f32[200,1]{0,1:T(1,128)}, u32[]{:S(2)}) copy-start(f32[200,1]{0,1:T(1,128)} %copy.74) | copy-start | bytes 2404
  96.9 10.7 %copy-start.40 = (f32[200,1]{0,1:T(1,128)S(1)}, f32[200,1]{0,1:T(1,128)}, u32[]{:S(2)}) copy-start(f32[200,1]{0,1:T(1,128)} %copy.73) | copy-start | bytes 2404
  96.9 10.7 %copy-start.41 = (f32[200,1]{0,1:T(1,128)S(1)}, f32[200,1]{0,1:T(1,128)}, u32[]{:S(2)}) copy-start(f32[200,1]{0,1:T(1,128)} %copy.72) | copy-start | bytes 2404
  96.9 10.7 %copy-start.42 = (f32[200,1]{0,1:T(1,128)S(1)}, f32[200,1]{0,1:T(1,128)}, u32[]{:S(2)}) copy-start(f32[200,1]{0,1:T(1,128)} %copy.60) | copy-start | bytes 2404
  96.9 10.7 %copy-start.43 = (f32[200,1]{0,1:T(1,128)S(1)}, f32[200,1]{0,1:T(1,128)}, u32[]{:S(2)}) copy-start(f32[200,1]{0,1:T(1,128)} %copy.107) | copy-start | bytes 2404
  96.9 10.7 %copy-start.44 = (f32[200,1]{0,1:T(1,128)S(1)}, f32[200,1]{0,1:T(1,128)}, u32[]{:S(2)}) copy-start(f32[200,1]{0,1:T(1,128)} %copy.106) | copy-start | bytes 2404
  97.0 10.7 %copy-start.45 = (f32[200,1]{0,1:T(1,128)S(1)}, f32[200,1]{0,1:T(1,128)}, u32[]{:S(2)}) copy-start(f32[200,1]{0,1:T(1,128)} %copy.105) | copy-start | bytes 2404
  97.0 10.7 %copy-start.46 = (f32[200,1]{0,1:T(1,128)S(1)}, f32[200,1]{0,1:T(1,128)}, u32[]{:S(2)}) copy-start(f32[200,1]{0,1:T(1,128)} %copy.104) | copy-start | bytes 2404
  97.0 10.7 %copy-start.47 = (f32[200,1]{0,1:T(1,128)S(1)}, f32[200,1]{0,1:T(1,128)}, u32[]{:S(2)}) copy-start(f32[200,1]{0,1:T(1,128)} %copy.103) | copy-start | bytes 2404
  97.0 10.7 %copy-start.48 = (f32[200,1]{0,1:T(1,128)S(1)}, f32[200,1]{0,1:T(1,128)}, u32[]{:S(2)}) copy-start(f32[200,1]{0,1:T(1,128)} %copy.102) | copy-start | bytes 2404
  97.0 10.7 %copy-start.49 = (f32[200,1]{0,1:T(1,128)S(1)}, f32[200,1]{0,1:T(1,128)}, u32[]{:S(2)}) copy-start(f32[200,1]{0,1:T(1,128)} %copy.101) | copy-start | bytes 2404
  97.0 10.7 %copy-start.50 = (f32[200,1]{0,1:T(1,128)S(1)}, f32[200,1]{0,1:T(1,128)}, u32[]{:S(2)}) copy-start(f32[200,1]{0,1:T(1,128)} %copy.100) | copy-start | bytes 2404
  97.0 10.7 %copy-start.51 = (f32[200,1]{0,1:T(1,128)S(1)}, f32[200,1]{0,1:T(1,128)}, u32[]{:S(2)}) copy-start(f32[200,1]{0,1:T(1,128)} %copy.99) | copy-start | bytes 2404
  97.0 10.7 %copy-start.52 = (f32[200,1]{0,1:T(1,128)S(1)}, f32[200,1]{0,1:T(1,128)}, u32[]{:S(2)}) copy-start(f32[200,1]{0,1:T(1,128)} %copy.98) | copy-start | bytes 2404
  97.0 10.7 %copy-start.53 = (f32[200,1]{0,1:T(1,128)S(1)}, f32[200,1]{0,1:T(1,128)}, u32[]{:S(2)}) copy-start(f32[200,1]{0,1:T(1,128)} %copy.97) | copy-start | bytes 2404
  97.0 10.7 %copy-start.54 = (f32[200,1]{0,1:T(1,128)S(1)}, f32[200,1]{0,1:T(1,128)}, u32[]{:S(2)}) copy-start(f32[200,1]{0,1:T(1,128)} %copy.96) | copy-start | bytes 2404
  97.1 10.7 %copy-start.55 = (f32[200,1]{0,1:T(1,128)S(1)}, f32[200,1]{0,1:T(1,128)}, u32[]{:S(2)}) copy-start(f32[200,1]{0,1:T(1,128)} %copy.95) | copy-start | bytes 2404
  106.3 11.0 %copy-start.14 = (bf16[800,200]{1,0:T(8,128)(2,1)}, bf16[800,200]{1,0:T(8,128)(2,1)S(1)}, u32[]{:S(2)}) copy-start(bf16[800,200]{1,0:T(8,128)(2,1)S(1)} %all_gather.18) | copy-start | bytes 960004
  117.3 78.7 %copy-start.62 = (s32[77]{0:T(128)S(1)}, s32[77]{0:T(128)}, u32[]{:S(2)}) copy-start(s32[77]{0:T(128)} %param.12) | copy-start | bytes 928
  219.9 17.9 %copy-start.2 = (bf16[1,800,8,128]{3,1,2,0:T(8,128)(2,1)S(1)}, bf16[1,800,8,128]{3,1,2,0:T(8,128)(2,1)}, u32[]{:S(2)}) copy-start(bf16[1,800,8,128]{3,1,2,0:T(8,128)(2,1)} %copy-done.1) | copy-start | bytes 4915204
  220.8 731.2 %all-reduce.15.cloned.1.call-start = ((), (), s32[]{:S(2)}) async-start(), calls=%async_computation.2 | async-start | bytes 811008 | tf_op jit(solution)/shard_map/psum | solution.py:147
  220.9 18.5 %collective-permute-start.3 = (bf16[1,200,6,128]{3,1,2,0:T(8,128)(2,1)}, bf16[1,200,6,128]{3,1,2,0:T(8,128)(2,1)S(1)}, u32[]{:S(2)}, u32[]{:S(2)}) collective-permute-start(bf16[1,200,6,128]{3,1,2,0:T(8,128)(2,1)} %get-tuple-element.100), channel_id=1, source_target_pairs={{4,0},{8,4},{12,8},{16,12},{20,16},{24,20},{28,24},{32,28},{36,32}... | collective-permute-start | bytes 921608 | tf_op jit(solution)/shard_map/ppermute | solution.py:23
  225.3 14.8 %collective-permute-start.2 = (bf16[1,200,6,128]{3,1,2,0:T(8,128)(2,1)}, bf16[1,200,6,128]{3,1,2,0:T(8,128)(2,1)S(1)}, u32[]{:S(2)}, u32[]{:S(2)}) collective-permute-start(bf16[1,200,6,128]{3,1,2,0:T(8,128)(2,1)} %get-tuple-element.101), channel_id=1, source_target_pairs={{0,4},{4,8},{8,12},{12,16},{16,20},{20,24},{24,28},{28,32},{32,36}... | collective-permute-start | bytes 921608 | tf_op jit(solution)/shard_map/ppermute | solution.py:21
  241.2 26.0 %copy-start.17 = (f32[200,49]{0,1:T(8,128)S(1)}, f32[200,49]{0,1:T(8,128)}, u32[]{:S(2)}) copy-start(f32[200,49]{0,1:T(8,128)} %stack.199) | copy-start | bytes 117604
  265.3 18.3 %collective-permute-start.5 = (f32[42,800]{1,0:T(8,128)S(1)}, f32[42,800]{1,0:T(8,128)S(1)}, u32[]{:S(2)}, u32[]{:S(2)}) collective-permute-start(f32[42,800]{1,0:T(8,128)S(1)} %slice.876), channel_id=1, source_target_pairs={{0,1},{1,2},{2,3},{4,5},{5,6},{6,7},{8,9},{9,10},{10,11},{12,13},{... | collective-permute-start | bytes 403208
  279.7 6.5 collective-permute-start.6
  281.6 5.1 collective-permute-start.4
  (24 other events, 145.4 us)
Sparse Core Ops, SparseCore 0:
  220.9 16.6 reduce-scatter.8
  284.7 667.2 all-reduce.14
where the time goes:
time: 964 us; the launch traced here: 962 us
  blocking collectives  491 us (51%)
  waiting for transfers between devices  306 us (32%)
  local copies, waits for them, and re-layouts  75.4 us (8%)
  other arithmetic  35.1 us (4%)
  starting transfers between devices  19.5 us (2%)
  matrix products  17.5 us (2%)
  between operations  16.9 us (2%)
    psum x1, blocking collectives, shards(): lax.psum((local_gradients[0], local_gradients[1], local_gradients[2], loc...  359 us
    psum x1, waiting for transfers between devices, shards(): lax.psum((local_gradients[0], local_gradients[1], local_gradients[2], loc...  305 us
    psum x1, blocking collectives, shards(): squares, ocean_count = lax.psum((squares, ocean_local), ('lon', 'dp'))  75.7 us
    unnamed x193, local copies, waits for them, and re-layouts  60.1 us
    unnamed x2, blocking collectives  26.7 us
  transfers between devices with their start and end apart: 9, of which 3 were waited for; matrix products, arithmetic and copies ran while one was open for 10% of the time, Pallas kernels for 0%

commit v1 on v0

v1 whole, which is shorter than its diff:
```python
import jax
import jax.numpy as jnp
from jax import lax
from jax.experimental import pallas as pl
from jax.experimental.pallas import tpu as pltpu
from jax.sharding import PartitionSpec as P

MESH = pl.DeviceIdType.MESH
F32 = jnp.float32
BF16 = jnp.bfloat16

V = 77
VP = 80
C = 200
CP = 256
FF = 800
FP = 896
FB = 160
COLS = 8
LAT = 128
SIDE = 7
HALO = 6
SLOTS = COLS + 2 * HALO
CELLS = COLS * LAT
GELU_K = 0.7978845608


def dot(a, b):
    return jnp.dot(a, b, preferred_element_type=F32)


def dot_nt(a, b):
    return lax.dot_general(a, b, (((1,), (1,)), ((), ())), preferred_element_type=F32)


def remote(src, dst, send, recv, device):
    return pltpu.make_async_remote_copy(
        src_ref=src,
        dst_ref=dst,
        send_sem=send,
        recv_sem=recv,
        device_id=device,
        device_id_type=MESH,
    )


def padded_row(channel):
    step = (channel >= 50).astype(jnp.int32)
    step += (channel >= 100).astype(jnp.int32)
    step += (channel >= 150).astype(jnp.int32)
    return channel + 14 * step


def body(
    fields, targets, land, clip, stem, dw, up, down, head,
    o_stem, o_kern, o_up, o_down, o_head, o_loss, o_sens,
    f32a, f32b, fbuf, fm, wp, wd, ga, gb, gd,
    stem_w, stem_t, kern_w, up_w, up_t, head_w, head_t, down_w, down_t, down_f,
    xs, ms, nh, nhp, act, slope, pre, bo, mis, sq, sa, sb,
    bg, bh, gdn, gup, back, sh, small, smp,
    ld, lu, rd0, ru0, ls1, rx1, s2, rx2, fin, lg,
    stx, srx, s2x, sfin, sen, hl, hr,
    send_g, recv_g, send_h, recv_h, send_s, recv_s,
):
    lon = lax.axis_index("lon")
    dp = lax.axis_index("dp")
    x_hi, y, z = lon // 32, (lon // 8) % 4, lon % 8
    x_lo, core = dp // 2, dp % 2
    right = ((lon + 1) % 64, dp)
    left = ((lon + 63) % 64, dp)
    sibling = (lon, x_lo * 2 + (1 - core))
    idx_a = y * 4 + dp
    idx_b = x_hi * 8 + z
    idx_c = x_lo * 4 + y

    def peer_a(k):
        j = (idx_a + k) % 16
        return j, (x_hi * 32 + (j // 4) * 8 + z, j % 4)

    def peer_b(k):
        j = (idx_b + k) % 16
        return j, ((j // 8) * 32 + y * 8 + j % 8, dp)

    def peer_c(k):
        j = (idx_c + k) % 8
        return j, (x_hi * 32 + (j % 4) * 8 + z, (j // 4) * 2 + core)

    def peer_y(k):
        j = (y + k) % 4
        return j, (x_hi * 32 + j * 8 + z, dp)

    barrier = pltpu.get_barrier_semaphore()
    for target in (right, left):
        pl.semaphore_signal(barrier, inc=1, device_id=target, device_id_type=MESH)
    for k in range(1, 16):
        pl.semaphore_signal(barrier, inc=1, device_id=peer_a(k)[1], device_id_type=MESH)
        pl.semaphore_signal(barrier, inc=1, device_id=peer_b(k)[1], device_id_type=MESH)

    f32a[0 : V * COLS, :] = fields[...].astype(F32).reshape(V * COLS, LAT)
    f32a[V * COLS : VP * COLS, :] = jnp.zeros(((VP - V) * COLS, LAT), F32)
    f32b[0 : V * COLS, :] = targets[...].astype(F32).reshape(V * COLS, LAT)
    f32b[V * COLS : VP * COLS, :] = jnp.zeros(((VP - V) * COLS, LAT), F32)
    for i in range(COLS):
        fbuf[HALO + i] = f32a[pl.ds(i, VP, stride=COLS), :].astype(BF16)
    wp[...] = jnp.zeros(wp.shape, F32)
    wp[0:50, 0:V] = stem[...].astype(F32)
    wp[0:50, 128:177] = dw[...].astype(F32)
    wp[0:50, 256 : 256 + FF] = up[...].astype(F32)
    wp[0:50, 256 + FP : 256 + FP + V] = head[...].astype(F32)
    wd[...] = jnp.zeros(wd.shape, F32)
    wd[0:C, 0:C] = down[...].astype(F32)
    ga[dp] = wp[:, 0:256].astype(BF16)
    gb[dp] = wp[:, 256 : 256 + FP + 128].astype(BF16)
    gd[dp] = wd[...].astype(BF16)

    pl.semaphore_wait(barrier, 32)

    halo = [
        remote(fbuf.at[pl.ds(8, 6)], fbuf.at[pl.ds(0, 6)], send_h.at[0], recv_h.at[0], right),
        remote(fbuf.at[pl.ds(6, 6)], fbuf.at[pl.ds(14, 6)], send_h.at[1], recv_h.at[1], left),
    ]
    gathers = []
    for a, buf in enumerate((ga, gb, gd)):
        group = []
        for k in range(1, 4):
            group.append(
                remote(
                    buf.at[dp], buf.at[dp], send_g.at[a * 3 + k - 1], recv_g.at[a * 3 + k - 1],
                    (lon, (dp + k) % 4),
                )
            )
        gathers.append(group)
    for copy in gathers[0]:
        copy.start()
    for copy in halo:
        copy.start()
    for copy in gathers[1] + gathers[2]:
        copy.start()

    def stage(index, count, peers, src, dst):
        for k in range(1, count):
            j, device = peers(k)
            remote(src(j), dst, send_s.at[index], recv_s.at[index], device).start()

    def stage_wait(index, count, buf):
        whole = buf.at[pl.ds(0, count - 1)]
        both = remote(whole, whole, send_s.at[index], recv_s.at[index], right)
        both.wait_recv()
        both.wait_send()

    row = lax.broadcasted_iota(jnp.int32, (CP, CP), 0)
    col = lax.broadcasted_iota(jnp.int32, (CP, CP), 1)
    from_padded = jnp.where((row < C) & (col == padded_row(row)), 1.0, 0.0).astype(BF16)
    to_padded = jnp.where((col < C) & (row == padded_row(col)), 1.0, 0.0).astype(BF16)
    lane = lax.broadcasted_iota(jnp.int32, (8, LAT), 1)
    keep = {b: (lane + b >= 0) & (lane + b < LAT) for b in range(-HALO, HALO + 1, 2)}

    for i in range(COLS):
        fm[:, (HALO + i) * LAT : (HALO + i + 1) * LAT] = fbuf[HALO + i]

    for copy in gathers[0]:
        copy.wait_recv()
    first = dot(from_padded, ga[...].reshape(CP, 256))
    stem_w[...] = first[:, 0:128].astype(BF16)
    stem_t[...] = first[:, 0:128].T.astype(BF16)
    kern_w[...] = first[0:C, 128:256]

    def stem_pair(s):
        out = dot(stem_w[:, 0:VP], fm[:, s * LAT : (s + 2) * LAT])[0:C].astype(BF16).astype(F32)
        xs[s] = out[:, 0:LAT]
        xs[s + 1] = out[:, LAT : 2 * LAT]

    for s in range(HALO, HALO + COLS, 2):
        stem_pair(s)
    for copy in halo:
        copy.wait_recv()
    for s in list(range(0, HALO)) + list(range(HALO + COLS, SLOTS)):
        fm[:, s * LAT : (s + 1) * LAT] = fbuf[s]
    for s in list(range(0, HALO, 2)) + list(range(HALO + COLS, SLOTS, 2)):
        stem_pair(s)

    def conv_forward(block, carry):
        here = pl.ds(pl.multiple_of(block * 8, 8), 8)
        x = [xs[s, here, :] for s in range(SLOTS)]
        weights = kern_w[here, :]
        out = [None] * COLS
        for q in range(SIDE):
            b = (q - 3) * 2
            w = [
                jnp.broadcast_to(weights[:, p * SIDE + q : p * SIDE + q + 1], (8, LAT))
                for p in range(SIDE)
            ]
            for i in range(COLS):
                total = w[0] * x[i]
                for p in range(1, SIDE):
                    total = total + w[p] * x[i + 2 * p]
                if b != 0:
                    total = jnp.where(keep[b], pltpu.roll(total, (-b) % LAT, 1), 0.0)
                out[i] = total if out[i] is None else out[i] + total
        for i in range(COLS):
            ms[i, here, :] = out[i]
        return carry

    lax.fori_loop(0, C // 8, conv_forward, 0)

    nh[...] = jnp.zeros(nh.shape, BF16)
    rstds = []
    for i in range(COLS):
        tile = ms[i]
        centred = tile - jnp.mean(tile, axis=0, keepdims=True)
        rstd = lax.rsqrt(jnp.mean(centred * centred, axis=0, keepdims=True) + 1e-06)
        normed = centred * rstd
        ms[i] = normed
        rstds.append(rstd)
        nh[0:C, i * LAT : (i + 1) * LAT] = normed.astype(BF16)

    for copy in gathers[1]:
        copy.wait_recv()
    second = dot(from_padded, gb[...].reshape(CP, FP + 128))
    up_w[...] = second[:, 0:FP].astype(BF16)
    up_t[...] = second[:, 0:FP].T.astype(BF16)
    head_w[...] = second[:, FP : FP + 128]
    head_t[...] = second[:, FP : FP + 128].T.astype(BF16)
    for copy in gathers[2]:
        copy.wait_recv()
    for d in range(4):
        down_f[C * d : C * (d + 1), :] = gd[d].astype(F32)[0:C]
    down_w[...] = down_f[...].astype(BF16)
    down_t[...] = down_f[...].T.astype(BF16)

    sq[...] = jnp.zeros(sq.shape, F32)
    bo[...] = jnp.zeros(bo.shape, BF16)
    for j in range(COLS // 2):
        part = pl.ds(j * 2 * LAT, 2 * LAT)
        for f in range(0, FF, FB):
            u = dot(up_t[f : f + FB, :], nh[:, part])
            u2 = u * u
            half = 0.5 + 0.5 * jnp.tanh(u * (GELU_K + (GELU_K * 0.044715) * u2))
            value = u * half
            act[f : f + FB, part] = value.astype(BF16)
            slope[f : f + FB, part] = half + value * (1.0 - half) * (
                2.0 * GELU_K + (6.0 * GELU_K * 0.044715) * u2
            )
        branch = dot(down_t[...], act[:, part])[0:C]
        centre = jnp.concatenate([xs[HALO + 2 * j], xs[HALO + 2 * j + 1]], axis=1)
        bo[0:C, part] = (centre + branch).astype(BF16)
        predicted = dot(head_t[0:VP, :], bo[:, part])
        for h in range(2):
            i = 2 * j + h
            ocean = land[i : i + 1, :].astype(F32)
            wanted = f32b[pl.ds(i, VP, stride=COLS), :]
            miss = (predicted[:, h * LAT : (h + 1) * LAT] - wanted) * ocean
            mis[:, i * LAT : (i + 1) * LAT] = miss.astype(BF16)
            sq[0:VP, :] = sq[0:VP, :] + miss * miss

    lanes = lax.broadcasted_iota(jnp.int32, (1, LAT), 1)
    ocean_local = jnp.sum(land[...].astype(F32))
    mine = jnp.sum(sq[...].T, axis=0, keepdims=True)
    sa[idx_a] = jnp.where(lanes == V, ocean_local, mine)
    stage(0, 16, peer_a, lambda j: sa.at[idx_a], sa.at[idx_a])

    nhp[...] = dot(to_padded, nh[...]).astype(BF16)
    small[:, 128:256] = jnp.zeros((CP, 128), F32)
    small[:, 128 : 128 + VP] = dot_nt(bo[...], mis[...])

    stage_wait(0, 16, sa)
    total = sa[0]
    for j in range(1, 16):
        total = total + sa[j]
    sb[idx_b] = total
    stage(1, 16, peer_b, lambda j: sb.at[idx_b], sb.at[idx_b])
    stage_wait(1, 16, sb)
    total = sb[0]
    for j in range(1, 16):
        total = total + sb[j]
    ocean_count = jnp.sum(jnp.where(lanes == V, total, 0.0), axis=1, keepdims=True)
    valid = lanes < V
    threshold = jnp.where(valid, clip[...].astype(F32) / 16.0, 1.0)
    mean_error = jnp.where(valid, total, 0.0) / ocean_count
    ratio = 1.0 + mean_error / threshold
    o_loss[...] = jnp.sum(jnp.where(valid, threshold * jnp.log(ratio), 0.0), axis=1, keepdims=True)
    factor = jnp.where(valid, 2.0 / (ocean_count * ratio), 0.0)

    small[:, 128:256] = small[:, 128:256] * factor
    scaled = (head_w[...] * factor).astype(BF16)
    for j in range(COLS // 2):
        part = pl.ds(j * 2 * LAT, 2 * LAT)
        grad = dot(scaled[:, 0:VP], mis[:, part])
        bg[:, part] = grad[0:C]
        bh[:, part] = grad.astype(BF16)
    gdn[FF : FF + 64, :] = jnp.zeros((64, CP), F32)
    for f in range(0, FF, FB):
        gdn[f : f + FB, :] = dot_nt(act[f : f + FB, :], bh[...])
    for d in range(4):
        for s in range(4):
            piece = (d % 2) * 8 + (d // 2) * 4 + s
            block = gdn[C * d + 64 * s : C * d + 64 * s + 64, :]
            ld[piece, 0:64, :] = block[:, 0:128].astype(BF16)
            ld[piece, 64:128, :] = block[:, 128:256].astype(BF16)
    away = pl.ds((1 - core) * 8, 8)
    copy_d = remote(ld.at[away], rd0, send_s.at[2], recv_s.at[2], sibling)
    copy_d.start()

    pre[FF:FP, :] = jnp.zeros((FP - FF, CELLS), BF16)
    for j in range(COLS // 2):
        part = pl.ds(j * 2 * LAT, 2 * LAT)
        for f in range(0, FF, FB):
            pre[f : f + FB, part] = (
                dot(down_w[f : f + FB, :], bh[:, part]) * slope[f : f + FB, part]
            ).astype(BF16)
    gup[...] = dot_nt(nhp[...], pre[...])
    for d in range(4):
        for s in range(4):
            piece = (d % 2) * 8 + (d // 2) * 4 + s
            for l in range(7):
                lu[piece, 16 * l : 16 * l + 16, :] = gup[
                    64 * d + 16 * s : 64 * d + 16 * s + 16, 128 * l : 128 * l + 128
                ].astype(BF16)
            lu[piece, 112:128, :] = jnp.zeros((16, 128), BF16)
    copy_u = remote(lu.at[away], ru0, send_s.at[3], recv_s.at[3], sibling)
    copy_u.start()

    for j in range(COLS // 2):
        part = pl.ds(j * 2 * LAT, 2 * LAT)
        grad = dot(up_w[...], pre[:, part])[0:C]
        for h in range(2):
            i = 2 * j + h
            g = grad[:, h * LAT : (h + 1) * LAT]
            normed = ms[i]
            mean_g = jnp.mean(g, axis=0, keepdims=True)
            mean_gn = jnp.mean(g * normed, axis=0, keepdims=True)
            ms[i] = (rstds[i] * (g - mean_g - normed * mean_gn)).astype(BF16).astype(F32)

    copy_d.wait_recv()
    copy_u.wait_recv()
    for j in range(8):
        ls1[j, 0:128, :] = (ld[core * 8 + j].astype(F32) + rd0[j].astype(F32)).astype(BF16)
        ls1[j, 128:256, :] = (lu[core * 8 + j].astype(F32) + ru0[j].astype(F32)).astype(BF16)
    stage(4, 8, peer_c, lambda j: ls1.at[j], rx1.at[idx_c])

    def conv_backward(block, carry):
        here = pl.ds(pl.multiple_of(block * 8, 8), 8)
        x = [xs[s, here, :] for s in range(SLOTS)]
        m = [ms[i, here, :] for i in range(COLS)]
        weights = kern_w[here, :]
        out = [None] * SLOTS
        kern = jnp.zeros((8, LAT), F32)
        for q in range(SIDE):
            b = (q - 3) * 2
            if b != 0:
                shifted = [jnp.where(keep[-b], pltpu.roll(t, b % LAT, 1), 0.0) for t in m]
            else:
                shifted = m
            for p in range(SIDE):
                t = p * SIDE + q
                w = jnp.broadcast_to(weights[:, t : t + 1], (8, LAT))
                corr = None
                for i in range(COLS):
                    s = i + 2 * p
                    term = w * shifted[i]
                    out[s] = term if out[s] is None else out[s] + term
                    prod = shifted[i] * x[s]
                    corr = prod if corr is None else corr + prod
                kern = jnp.where(lane == V + t, jnp.sum(corr, axis=1, keepdims=True), kern)
        for s in range(SLOTS):
            back[s, here, :] = out[s]
        small[here, 128:256] = small[here, 128:256] + kern
        return carry

    lax.fori_loop(0, C // 8, conv_backward, 0)

    stage_wait(4, 8, rx1)
    rx1[idx_c] = ls1[idx_c]
    large = rx1[0].astype(F32)
    for j in range(1, 8):
        large = large + rx1[j].astype(F32)
    s2[...] = large.astype(BF16).reshape(16, 16, 128)
    stage(5, 16, peer_b, lambda j: s2.at[j], rx2.at[idx_b])

    sh[C:CP, :] = jnp.zeros((CP - C, SLOTS * LAT), BF16)
    for s in range(SLOTS):
        value = back[s]
        if HALO <= s < HALO + COLS:
            value = value + bg[:, (s - HALO) * LAT : (s - HALO + 1) * LAT]
        sh[0:C, s * LAT : (s + 1) * LAT] = value.astype(BF16)
    small[:, 0:128] = jnp.zeros((CP, 128), F32)
    small[:, 0:VP] = dot_nt(sh[...], fm[...])
    smp[...] = dot(to_padded, small[...].astype(BF16)).astype(BF16)
    for d in range(4):
        for s in range(4):
            at = 64 * d + 16 * s
            stx[s * 4 + d, 0:16, :] = smp[at : at + 16, 0:128]
            stx[s * 4 + d, 16:32, :] = smp[at : at + 16, 128:256]
    stage(6, 16, peer_a, lambda j: stx.at[j], srx.at[idx_a])

    for s in list(range(0, HALO, 2)) + list(range(HALO + COLS, SLOTS, 2)):
        value = dot(stem_t[0:VP, :], sh[:, s * LAT : (s + 2) * LAT]).astype(BF16)
        sen[s if s < HALO else s - COLS] = value[:, 0:LAT]
        sen[s + 1 if s < HALO else s + 1 - COLS] = value[:, LAT : 2 * LAT]
    copy_l = remote(sen.at[pl.ds(0, 6)], hr, send_h.at[2], recv_h.at[2], left)
    copy_r = remote(sen.at[pl.ds(6, 6)], hl, send_h.at[3], recv_h.at[3], right)
    copy_l.start()
    copy_r.start()

    stage_wait(5, 16, rx2)
    rx2[idx_b] = s2[idx_b]
    part_sum = rx2[0].astype(F32)
    for j in range(1, 16):
        part_sum = part_sum + rx2[j].astype(F32)
    fin[idx_b] = part_sum.astype(BF16)
    stage(7, 16, peer_b, lambda j: fin.at[idx_b], fin.at[idx_b])

    stage_wait(6, 16, srx)
    srx[idx_a] = stx[idx_a]
    tiny = srx[0].astype(F32)
    for j in range(1, 16):
        tiny = tiny + srx[j].astype(F32)
    s2x[idx_b] = tiny.astype(BF16)
    stage(8, 16, peer_b, lambda j: s2x.at[idx_b], s2x.at[idx_b])

    stage_wait(7, 16, fin)
    lg[y] = fin[...].reshape(256, 128)
    stage(9, 4, peer_y, lambda j: lg.at[y], lg.at[y])

    stage_wait(8, 16, s2x)
    tiny = s2x[0].astype(F32)
    for j in range(1, 16):
        tiny = tiny + s2x[j].astype(F32)
    sfin[y] = tiny.astype(BF16)
    stage(10, 4, peer_y, lambda j: sfin.at[y], sfin.at[y])

    copy_l.wait_recv()
    copy_r.wait_recv()
    for j in range(COLS // 2):
        s = HALO + 2 * j
        value = dot(stem_t[0:VP, :], sh[:, s * LAT : (s + 2) * LAT])
        for h in range(2):
            i = 2 * j + h
            cells = value[:, h * LAT : (h + 1) * LAT]
            if i >= 2:
                cells = cells + hr[i - 2].astype(F32)
            if i < 6:
                cells = cells + hl[i].astype(F32)
            o_sens[pl.ds(i, V, stride=COLS), :] = (cells * ocean_count)[0:V]

    stage_wait(9, 4, lg)
    for s in range(4):
        rows = 16 if s < 3 else 2
        for l in range(7):
            width = min(128, FF - 128 * l)
            piece = lg[s, 128 + 16 * l : 144 + 16 * l, :].astype(F32)
            o_up[16 * s : 16 * s + rows, 128 * l : 128 * l + width] = piece[0:rows, 0:width]
        rows = 64 if s < 3 else 8
        piece = lg[s, 0:128, :].astype(F32)
        o_down[64 * s : 64 * s + rows, 0:128] = piece[0:rows]
        o_down[64 * s : 64 * s + rows, 128:C] = piece[64 : 64 + rows, 0 : C - 128]
    stage_wait(10, 4, sfin)
    for s in range(4):
        rows = 16 if s < 3 else 2
        piece = sfin[s].astype(F32)
        o_stem[16 * s : 16 * s + rows, :] = piece[0:rows, 0:V]
        o_head[16 * s : 16 * s + rows, :] = piece[16 : 16 + rows, 0:V]
        o_kern[16 * s : 16 * s + rows, :] = pltpu.roll(piece[16:32], LAT - V, 1)[0:rows, 0:49]

    for copy in gathers[0] + gathers[1] + gathers[2] + halo:
        copy.wait_send()
    for copy in (copy_d, copy_u, copy_l, copy_r):
        copy.wait_send()


SCRATCH = [
    ((VP * COLS, LAT), F32),
    ((VP * COLS, LAT), F32),
    ((SLOTS, VP, LAT), BF16),
    ((VP, SLOTS * LAT), BF16),
    ((64, 256 + FP + 128), F32),
    ((208, CP), F32),
    ((4, 64, 256), BF16),
    ((4, 64, FP + 128), BF16),
    ((4, 208, CP), BF16),
    ((CP, 128), BF16),
    ((128, CP), BF16),
    ((C, 128), F32),
    ((CP, FP), BF16),
    ((FP, CP), BF16),
    ((CP, 128), F32),
    ((128, CP), BF16),
    ((FF, CP), BF16),
    ((CP, FF), BF16),
    ((FF, CP), F32),
    ((SLOTS, C, LAT), F32),
    ((COLS, C, LAT), F32),
    ((CP, CELLS), BF16),
    ((CP, CELLS), BF16),
    ((FF, CELLS), BF16),
    ((FF, CELLS), F32),
    ((FP, CELLS), BF16),
    ((CP, CELLS), BF16),
    ((VP, CELLS), BF16),
    ((128, LAT), F32),
    ((16, 1, LAT), F32),
    ((16, 1, LAT), F32),
    ((C, CELLS), F32),
    ((CP, CELLS), BF16),
    ((FF + 64, CP), F32),
    ((CP, FP), F32),
    ((SLOTS, C, LAT), F32),
    ((CP, SLOTS * LAT), BF16),
    ((CP, 256), F32),
    ((CP, 256), BF16),
    ((16, 128, 128), BF16),
    ((16, 128, 128), BF16),
    ((8, 128, 128), BF16),
    ((8, 128, 128), BF16),
    ((8, 256, 128), BF16),
    ((8, 256, 128), BF16),
    ((16, 16, 128), BF16),
    ((16, 16, 128), BF16),
    ((16, 16, 128), BF16),
    ((4, 256, 128), BF16),
    ((16, 32, 128), BF16),
    ((16, 32, 128), BF16),
    ((16, 32, 128), BF16),
    ((4, 32, 128), BF16),
    ((12, VP, LAT), BF16),
    ((6, VP, LAT), BF16),
    ((6, VP, LAT), BF16),
]


def shards(
    fields, targets, land_sea, clip_level, stem_weight, dw_kernel, up_weight, down_weight, head_weight
):
    clip = jnp.pad(clip_level.reshape(1, V), ((0, 0), (0, LAT - V)), constant_values=16)
    shapes = [(50, V), (50, 49), (50, FF), (C, C), (50, V), (1, 1), (V * COLS, LAT)]
    vmem = pl.BlockSpec(memory_space=pltpu.VMEM)
    dma = pltpu.SemaphoreType.DMA
    outs = pl.pallas_call(
        body,
        out_shape=[jax.ShapeDtypeStruct(s, F32) for s in shapes],
        in_specs=[vmem] * 9,
        out_specs=[vmem] * 7,
        scratch_shapes=[pltpu.VMEM(s, t) for s, t in SCRATCH]
        + [dma((9,)), dma((9,)), dma((4,)), dma((4,)), dma((11,)), dma((11,))],
        compiler_params=pltpu.CompilerParams(
            collective_id=0, has_side_effects=True, vmem_limit_bytes=58 * 1024 * 1024
        ),
    )(
        fields.reshape(V, COLS, LAT),
        targets.reshape(V, COLS, LAT),
        land_sea,
        clip,
        stem_weight,
        dw_kernel,
        up_weight,
        down_weight,
        head_weight,
    )
    return (
        outs[0], outs[1], outs[2], outs[3], outs[4],
        outs[5].reshape(()),
        outs[6].reshape(1, V, COLS, LAT),
    )


def solution(mesh):
    placed = (
        P("dp", None, "lon", None),
        P("dp", None, "lon", None),
        P("lon", None),
        P(),
        P("dp", None),
        P("dp", None),
        P("dp", None),
        P("dp", None),
        P("dp", None),
    )
    return jax.shard_map(
        shards,
        mesh=mesh,
        in_specs=placed,
        out_specs=(
            P("dp", None),
            P("dp", None),
            P("dp", None),
            P("dp", None),
            P("dp", None),
            P(),
            P("dp", None, "lon", None),
        ),
        check_vma=False,
    )
```

time: 964 us -> 96.2 us (0.10)
  blocking collectives: 491 us -> 0 us
  waiting for transfers between devices: 306 us -> 0 us
  Pallas kernels: 0 us -> 85.5 us
  local copies, waits for them, and re-layouts: 75.4 us -> 6.88 us
  other arithmetic: 35.1 us -> 0 us
  starting transfers between devices: 19.5 us -> 0 us
  matrix products: 17.5 us -> 0 us
  between operations: 16.9 us -> 2.43 us
    psum x2 -> x0, blocking collectives: 435 us -> none  [the longest x1 359 us: shards(): lax.psum((local_gradients[0], local_gradients[1], local_gradients[2], loc...]
    psum x1 -> x0, waiting for transfers between devices: 305 us -> none  [shards(): lax.psum((local_gradients[0], local_gradients[1], local_gradients[2], loc...]
    pallas_call x0 -> x1, Pallas kernels: none -> 85.5 us  [shards(): pl.pallas_call(body, out_shape=[jax.ShapeDtypeStruct(s, F32) for s in sha...]
    unnamed x193 -> x16, local copies, waits for them, and re-layouts: 60.1 us -> 6.37 us
    all_gather x5 -> x0, blocking collectives: 29.8 us -> none  [the longest x1 6.82 us: shards(): lax.all_gather(up_weight, 'dp', axis=0, tiled=True)]
    unnamed x2 -> x0, blocking collectives: 26.7 us -> none
    reduce_sum x8 -> x0, other arithmetic: 23 us -> none  [the longest x4 13 us: shards(): jnp.sum(mixed_wide * kernel_window(padded, HALO + lon_off, HALO + lat_off...]
    dot_general x12 -> x0, matrix products: 17.5 us -> none  [the longest x1 4.35 us: shards(): jnp.einsum('fc,scla->sfla', down_full, block_half, preferred_element_type...]
  transfers between devices with their start and end apart: 9 -> 0, of which waited for: 3 -> 0; matrix products, arithmetic and copies ran while one was open for 10% -> 0% of each run, Pallas kernels for 0% -> 0%
where the time goes in v1:
time: 96.2 us; the launch traced here: 94.8 us
  Pallas kernels  85.5 us (89%)
  local copies, waits for them, and re-layouts  6.88 us (7%)
  between operations  2.43 us (3%)
    pallas_call x1, Pallas kernels, shards(): pl.pallas_call(body, out_shape=[jax.ShapeDtypeStruct(s, F32) for s in sha...  85.5 us
    unnamed x16, local copies, waits for them, and re-layouts  6.37 us

profile of v1, /device:TPU:6, one launch (start us, length us, event | category | flops | bytes accessed | tf_op | source)
XLA Modules:
  0.0 94.8 jit_solution(2959324882337097693)
XLA Ops:
  0.6 0.0 copy-start.4
  0.6 0.6 copy-done.4
  1.3 0.5 pad.4.clip
  1.8 85.5 %shard_map.144 = (f32[50,77]{1,0:T(8,128)}, f32[50,49]{1,0:T(8,128)}, f32[50,800]{1,0:T(8,128)}, f32[200,200]{1,0:T(8,128)}, f32[50,77]{1,0:T(8,128)}, /*index=5*/f32[1,1]{1,0:T(1,128)}, f32[616,128]{1,0:T(8,128)}) custom-call(bf16[77,8,128]{2,1,0:T(8,128)(2,1)} %bitcast.6, bf16[77,8,128]{2,1,0:T(8,128)(2,1)} %bitcast.7, s32[8,128]{1,0:T(8,128)} %land.1, ...), custom_call_target="tpu_custom_call" | custom-call | tf_op jit(solution)/shard_map/pallas_call | solution.py:538
  87.3 0.0 copy-start.3
  87.3 1.4 %copy.23 = f32[50,77]{1,0:T(8,128)} copy(f32[50,77]{1,0:T(8,128)} %get-tuple-element.28) | data formatting | bytes 30800
  88.6 0.0 copy-done.3
  88.6 0.6 copy.24
  89.3 0.0 copy-start.1
  89.3 1.7 %copy.25 = f32[50,800]{1,0:T(8,128)} copy(f32[50,800]{1,0:T(8,128)} %get-tuple-element.30) | data formatting | bytes 320000
  90.9 0.0 copy-done.1
  90.9 0.0 copy-start.2
  90.9 0.0 copy-start
  90.9 0.7 copy.26
  91.6 0.1 copy-done.2
  91.7 0.6 copy.27
  92.9 0.0 copy-done
  92.9 0.7 copy.29
Async XLA Ops:
  0.6 0.7 copy-start.4
  87.3 1.4 %copy-start.3 = (f32[50,49]{1,0:T(8,128)S(1)}, f32[50,49]{1,0:T(8,128)}, u32[]{:S(2)}) copy-start(f32[50,49]{1,0:T(8,128)} %get-tuple-element.29) | copy-start | bytes 29404
  89.3 1.7 %copy-start.1 = (f32[200,200]{1,0:T(8,128)S(1)}, f32[200,200]{1,0:T(8,128)}, u32[]{:S(2)}) copy-start(f32[200,200]{1,0:T(8,128)} %get-tuple-element.31) | copy-start | bytes 480004
  90.9 0.7 copy-start.2
  90.9 2.0 %copy-start = (f32[616,128]{1,0:T(8,128)S(1)}, f32[616,128]{1,0:T(8,128)}, u32[]{:S(2)}) copy-start(f32[616,128]{1,0:T(8,128)} %get-tuple-element.20) | copy-start | bytes 946180
